TPU v7x, 32 devices: a whole 2x2x4 slice. The times are simulated.
32 devices in a mesh: ctx: 8 (over y, x, core), tp: 4 (over z).
Axes of the slice: x: 2, y: 2, z: 4, core: 2. Of those that a mesh axis runs over, the one named last changes fastest.
Arguments:
- queries: bfloat16 [1, 8192, 4096], P(None, 'ctx', 'tp'), may hold values from -6 to 6
- keys: bfloat16 [1, 8192, 1024], P(None, 'ctx', 'tp'), may hold values from -6 to 6
- values: bfloat16 [1, 8192, 1024], P(None, 'ctx', 'tp'), may hold values from -6 to 6
- gates: int32 [1, 16, 8, 3], P(None, 'ctx', 'tp'), may hold values from 0 to 15, as said below
- out_weight: bfloat16 [4096, 4096], P('tp'), may hold values from -0.09375 to 0.09375
Outputs:
- projected: bfloat16 [1, 8192, 4096], P(None, 'ctx', 'tp')
Inputs may be any that keep to these rules, and one draw needn't show every extreme that they name: `gates`: for each sequence and key-value head, the 6 entries of query blocks 2 c to 2 c + 1 name blocks of 6 different values of (block // 2).
All inputs are finite; a program needn't handle non-finite values.
Results may differ from a plain program's by a relative error of at most 0.015.
Values may be sent and summed in bfloat16 or wider, within the bound.
A program may use at most 128 MiB of HBM per device.

v0:
```python
import functools

import jax
import jax.numpy as jnp
from jax import lax
from jax.experimental import pallas as pl
from jax.experimental.pallas import tpu as pltpu
from jax.sharding import PartitionSpec as P

MESH = pl.DeviceIdType.MESH
HD = 128
TOKB = 512
PICKS = 3
TILE = 128
PAIR = 2
FINAL_LAG = 3
LOW = -1e30
VMEM_LIMIT = 60 * 1024 * 1024


def kernel(
    n_ctx, n_tp, q_ref, k_ref, v_ref, gates_ref, w_hbm, out_ref,
    kbuf, vbuf, wbuf, att, part, from_left, from_right, acc,
    local_sem, w_sem, kv_send, kv_recv, rs_send, left_recv, right_recv,
):
    me = lax.axis_index("ctx")
    rank = lax.axis_index("tp")
    blocks = k_ref.shape[0]
    kv_heads = k_ref.shape[2] // HD
    group = q_ref.shape[1] // HD // kv_heads
    tiles = q_ref.shape[0] // TILE
    block_tiles = TOKB // TILE
    width = wbuf.shape[2]
    chips = n_ctx // 2
    chip, core = me // 2, me % 2
    sibling = chip * 2 + (1 - core)
    right = lax.rem(rank + 1, n_tp)
    left = lax.rem(rank + n_tp - 1, n_tp)

    for d in range(n_tp):
        pltpu.make_async_copy(
            w_hbm.at[:, pl.ds(d * width, width)], wbuf.at[d], w_sem.at[d]
        ).start()

    def slot(buf, device):
        return buf.at[pl.ds(device * blocks, blocks)]

    own = []
    for i, (src, buf) in enumerate(((k_ref, kbuf), (v_ref, vbuf))):
        copy = pltpu.make_async_copy(src, slot(buf, me), local_sem.at[i])
        copy.start()
        own.append(copy)

    barrier = pltpu.get_barrier_semaphore()
    for off in range(1, chips):
        peer = lax.rem(chip + off, chips) * 2 + core
        pl.semaphore_signal(barrier, inc=1, device_id={"ctx": peer}, device_id_type=MESH)
    pl.semaphore_signal(barrier, inc=1, device_id={"ctx": sibling}, device_id_type=MESH)

    @pl.when(rank > 0)
    def _():
        pl.semaphore_signal(barrier, inc=1, device_id={"tp": left}, device_id_type=MESH)

    @pl.when(rank < n_tp - 1)
    def _():
        pl.semaphore_signal(barrier, inc=1, device_id={"tp": right}, device_id_type=MESH)

    pl.semaphore_wait(
        barrier, chips + jnp.where(rank > 0, 1, 0) + jnp.where(rank < n_tp - 1, 1, 0)
    )

    def kv_copies(src_k, src_v, source, target, level, off):
        made = []
        for i, (src, buf) in enumerate(((src_k, kbuf), (src_v, vbuf))):
            made.append(
                pltpu.make_async_remote_copy(
                    src_ref=src,
                    dst_ref=slot(buf, source),
                    send_sem=kv_send.at[i, level, off],
                    recv_sem=kv_recv.at[i, source],
                    device_id={"ctx": target},
                    device_id_type=MESH,
                )
            )
        return made

    sent = []
    for off in range(1, chips):
        peer = lax.rem(chip + off, chips) * 2 + core
        for copy in kv_copies(k_ref, v_ref, me, peer, 0, off):
            copy.start()
            sent.append(copy)
    for copy in kv_copies(k_ref, v_ref, me, sibling, 1, 0):
        copy.start()
        sent.append(copy)
    for off in range(1, chips):
        source = lax.rem(chip + chips - off, chips) * 2 + core
        copies = kv_copies(slot(kbuf, source), slot(vbuf, source), source, sibling, 1, off)
        for copy in copies:
            copy.wait_recv()
            copy.start()
            sent.append(copy)
    for off in range(chips):
        source = lax.rem(chip + chips - off, chips) * 2 + (1 - core)
        for copy in kv_copies(slot(kbuf, source), slot(vbuf, source), source, sibling, 1, off):
            copy.wait_recv()
    for copy in own:
        copy.wait()
    for d in range(n_tp):
        pltpu.make_async_copy(
            w_hbm.at[:, pl.ds(d * width, width)], wbuf.at[d], w_sem.at[d]
        ).wait()

    def rs_copy(d, t, rightward):
        return pltpu.make_async_remote_copy(
            src_ref=part.at[d, t],
            dst_ref=(from_left if rightward else from_right).at[d, t],
            send_sem=rs_send.at[d, t],
            recv_sem=(left_recv if rightward else right_recv).at[d, t],
            device_id={"tp": right if rightward else left},
            device_id_type=MESH,
        )

    factor = HD ** (-0.5) * 1.4426950408889634
    pairs = group // PAIR

    def attend(t):
        b = t // block_tiles
        row0 = pl.multiple_of(t * TILE, TILE)
        in_block = (t % block_tiles) * TILE
        own_block = me * blocks + b

        def unit(i, carry):
            e = i // pairs
            lane0 = i * PAIR * HD
            kv_lane = pl.ds(pl.multiple_of(e * HD, HD), HD)
            lanes = [pl.ds(pl.multiple_of(lane0 + h * HD, HD), HD) for h in range(PAIR)]
            q = jnp.concatenate([q_ref[pl.ds(row0, TILE), lane] for lane in lanes], axis=0)
            index, bias = [own_block], [None]
            for j in range(PICKS):
                g = gates_ref[(b * kv_heads + e) * PICKS + j]
                valid = g < own_block
                index.append(jnp.where(valid, g, own_block))
                bias.append(jnp.where(valid, 0.0, LOW).astype(jnp.float32))
            scores = []
            for j in range(PICKS + 1):
                s = lax.dot_general(
                    q, kbuf[index[j], :, kv_lane], (((1,), (1,)), ((), ())),
                    preferred_element_type=jnp.float32,
                )
                if j == 0:
                    row = lax.broadcasted_iota(jnp.int32, s.shape, 0) % TILE + in_block
                    col = lax.broadcasted_iota(jnp.int32, s.shape, 1)
                    s = jnp.where(row >= col, s, LOW)
                else:
                    s = s + bias[j]
                scores.append(s)
            largest = functools.reduce(
                jnp.maximum, [jnp.max(s, axis=1, keepdims=True) for s in scores]
            )
            total, summed = 0.0, 0.0
            for j in range(PICKS + 1):
                raw = jnp.exp2((scores[j] - largest) * factor)
                total = total + jnp.sum(raw, axis=1, keepdims=True)
                summed = summed + jnp.dot(
                    raw.astype(jnp.bfloat16), vbuf[index[j], :, kv_lane],
                    preferred_element_type=jnp.float32,
                )
            result = (summed / total).astype(jnp.bfloat16)
            for h, lane in enumerate(lanes):
                att[:, lane] = result[h * TILE:(h + 1) * TILE]
            return carry

        lax.fori_loop(0, kv_heads * pairs, unit, 0)

    def project(t):
        def chunk(i, carry):
            d = jnp.where(rank < n_tp // 2, n_tp - 1 - i, i)
            part[d, t] = jnp.dot(
                att[...], wbuf[d], preferred_element_type=jnp.float32
            ).astype(jnp.bfloat16)

            @pl.when((rank == 0) & (d > 0))
            def _():
                rs_copy(d, t, True).start()

            @pl.when((rank == n_tp - 1) & (d < n_tp - 1))
            def _():
                rs_copy(d, t, False).start()

            return carry

        lax.fori_loop(0, n_tp, chunk, 0)

    def pass_on(t):
        def go_right(i, carry):
            d = n_tp - 1 - i

            @pl.when((d > rank) & (rank > 0))
            def _():
                copy = rs_copy(d, t, True)
                copy.wait_recv()
                part[d, t] = (
                    part[d, t].astype(jnp.float32) + from_left[d, t].astype(jnp.float32)
                ).astype(jnp.bfloat16)
                copy.start()

            return carry

        def go_left(d, carry):
            @pl.when((d < rank) & (rank < n_tp - 1))
            def _():
                copy = rs_copy(d, t, False)
                copy.wait_recv()
                part[d, t] = (
                    part[d, t].astype(jnp.float32) + from_right[d, t].astype(jnp.float32)
                ).astype(jnp.bfloat16)
                copy.start()

            return carry

        lax.fori_loop(0, n_tp, go_right, 0)
        lax.fori_loop(0, n_tp, go_left, 0)

    def finish(t):
        acc[...] = part[rank, t].astype(jnp.float32)

        @pl.when(rank > 0)
        def _():
            rs_copy(rank, t, True).wait_recv()
            acc[...] += from_left[rank, t].astype(jnp.float32)

        @pl.when(rank < n_tp - 1)
        def _():
            rs_copy(rank, t, False).wait_recv()
            acc[...] += from_right[rank, t].astype(jnp.float32)

        out_ref[pl.ds(pl.multiple_of(t * TILE, TILE), TILE), :] = acc[...].astype(jnp.bfloat16)

    def step(s, carry):
        @pl.when(s < tiles)
        def _():
            attend(s)
            project(s)

        @pl.when((s >= 1) & (s <= tiles))
        def _():
            pass_on(s - 1)

        @pl.when(s >= FINAL_LAG)
        def _():
            finish(s - FINAL_LAG)

        return carry

    lax.fori_loop(0, tiles + FINAL_LAG, step, 0)

    def drain(i, carry):
        d, t = i // tiles, i % tiles

        @pl.when(d != rank)
        def _():
            rs_copy(d, t, True).wait_send()

        return carry

    lax.fori_loop(0, n_tp * tiles, drain, 0)
    for copy in sent:
        copy.wait_send()


def per_device(n_ctx, n_tp, queries, keys, values, gates, out_weight):
    seqs, rows, q_width = queries.shape
    kv_width = keys.shape[2]
    blocks = rows // TOKB
    tiles = rows // TILE
    chips = n_ctx // 2
    depth, features = out_weight.shape
    width = features // n_tp
    vmem = pl.BlockSpec(memory_space=pltpu.VMEM)
    bf16 = jnp.bfloat16
    out = pl.pallas_call(
        functools.partial(kernel, n_ctx, n_tp),
        out_shape=jax.ShapeDtypeStruct((rows, width), bf16),
        in_specs=[
            vmem, vmem, vmem,
            pl.BlockSpec(memory_space=pltpu.SMEM),
            pl.BlockSpec(memory_space=pl.ANY),
        ],
        out_specs=vmem,
        scratch_shapes=[
            pltpu.VMEM((n_ctx * blocks, TOKB, kv_width), bf16),
            pltpu.VMEM((n_ctx * blocks, TOKB, kv_width), bf16),
            pltpu.VMEM((n_tp, depth, width), bf16),
            pltpu.VMEM((TILE, q_width), bf16),
            pltpu.VMEM((n_tp, tiles, TILE, width), bf16),
            pltpu.VMEM((n_tp, tiles, TILE, width), bf16),
            pltpu.VMEM((n_tp, tiles, TILE, width), bf16),
            pltpu.VMEM((TILE, width), jnp.float32),
            pltpu.SemaphoreType.DMA((2,)),
            pltpu.SemaphoreType.DMA((n_tp,)),
            pltpu.SemaphoreType.DMA((2, 2, chips)),
            pltpu.SemaphoreType.DMA((2, n_ctx)),
            pltpu.SemaphoreType.DMA((n_tp, tiles)),
            pltpu.SemaphoreType.DMA((n_tp, tiles)),
            pltpu.SemaphoreType.DMA((n_tp, tiles)),
        ],
        compiler_params=pltpu.CompilerParams(
            collective_id=0, has_side_effects=True, vmem_limit_bytes=VMEM_LIMIT
        ),
        cost_estimate=pl.CostEstimate(
            flops=4 * rows * q_width * (PICKS + 1) * TOKB + 2 * rows * depth * features,
            bytes_accessed=2 * (rows * q_width + 2 * rows * kv_width + depth * features),
            transcendentals=rows * (q_width // HD) * (PICKS + 1) * TOKB,
        ),
    )(
        queries.reshape(rows, q_width),
        keys.reshape(blocks, TOKB, kv_width),
        values.reshape(blocks, TOKB, kv_width),
        gates.reshape(-1),
        out_weight,
    )
    return out.reshape(seqs, rows, width)


def solution(mesh):
    placed = (
        P(None, "ctx", "tp"),
        P(None, "ctx", "tp"),
        P(None, "ctx", "tp"),
        P(None, "ctx", "tp", None),
        P("tp", None),
    )
    return jax.shard_map(
        functools.partial(per_device, mesh.shape["ctx"], mesh.shape["tp"]),
        mesh=mesh, in_specs=placed, out_specs=P(None, "ctx", "tp"), check_vma=False,
    )
```

profile of v0, /device:TPU:0, one launch (start us, length us, event | category | flops | bytes accessed | tf_op | source)
XLA Modules:
  0.0 225.4 jit_solution(5248199653467985731)
XLA Ops:
  0.0 1.3 reshape.18.gates_ref
  1.3 221.0 %shard_map.55 = bf16[1024,1024]{1,0:T(8,128)(2,1)} custom-call(bf16[1024,1024]{1,0:T(8,128)(2,1)} %bitcast.5, bf16[2,512,256]{2,1,0:T(8,128)(2,1)} %bitcast.6, bf16[2,512,256]{2,1,0:T(8,128)(2,1)} %bitcast.7, s32[12]{0:T(128)} %reshape.18.gates_ref, bf16[1024,4096]{1,0:T(8,128)(2,1)} %w_hbm.1), custom_call_target="tpu_custom_call" | custom-call | flops 17179869184 | bytes 11534336 | tf_op jit(solution)/shard_map/pallas_call | solution.py:282
  222.3 3.1 %copy.7 = bf16[1,1024,1024]{2,1,0:T(8,128)(2,1)} copy(bf16[1,1024,1024]{2,1,0:T(8,128)(2,1)} %bitcast.4) | data formatting | bytes 4194304
where the time goes:
time: 226 us; the launch traced here: 225 us
  Pallas kernels  221 us (98%)
  local copies, waits for them, and re-layouts  4.35 us (2%)
    pallas_call x1, Pallas kernels, per_device(): pl.pallas_call(functools.partial(kernel, n_ctx, n_tp), out_shape=jax.Shap...  221 us

commit v1 on v0

--- a/solution.py
+++ b/solution.py
@@ -1,4 +1,5 @@
 import functools
+import math
 
 import jax
 import jax.numpy as jnp
@@ -13,15 +14,16 @@
 PICKS = 3
 TILE = 128
 PAIR = 2
-FINAL_LAG = 3
+FIRST_FAR = 2
 LOW = -1e30
 VMEM_LIMIT = 60 * 1024 * 1024
 
 
 def kernel(
     n_ctx, n_tp, q_ref, k_ref, v_ref, gates_ref, w_hbm, out_ref,
-    kbuf, vbuf, wbuf, att, part, from_left, from_right, acc,
+    kbuf, vbuf, wbuf, w_far, att, att_far, part, from_left, from_right, acc,
     local_sem, w_sem, kv_send, kv_recv, rs_send, left_recv, right_recv,
+    att_send, att_recv, slice_send, slice_recv, far_send, far_recv, relay_send,
 ):
     me = lax.axis_index("ctx")
     rank = lax.axis_index("tp")
@@ -84,37 +86,162 @@
             )
         return made
 
-    sent = []
+    side = math.isqrt(chips)
+    x = chip % side
+
+    def peer_chip(off):
+        return lax.rem(chip + off, chips)
+
+    def diagonal(first, second):
+        return (first % side != second % side) & (first // side != second // side)
+
+    def start_all(copies):
+        for copy in copies:
+            copy.start()
+
+    def first_hop(off):
+        target = peer_chip(off)
+        return kv_copies(k_ref, v_ref, me, target * 2 + core, 0, off)
+
     for off in range(1, chips):
-        peer = lax.rem(chip + off, chips) * 2 + core
-        for copy in kv_copies(k_ref, v_ref, me, peer, 0, off):
-            copy.start()
-            sent.append(copy)
-    for copy in kv_copies(k_ref, v_ref, me, sibling, 1, 0):
-        copy.start()
-        sent.append(copy)
-    for off in range(1, chips):
-        source = lax.rem(chip + chips - off, chips) * 2 + core
-        copies = kv_copies(slot(kbuf, source), slot(vbuf, source), source, sibling, 1, off)
-        for copy in copies:
-            copy.wait_recv()
-            copy.start()
-            sent.append(copy)
-    for off in range(chips):
-        source = lax.rem(chip + chips - off, chips) * 2 + (1 - core)
-        for copy in kv_copies(slot(kbuf, source), slot(vbuf, source), source, sibling, 1, off):
-            copy.wait_recv()
-    for copy in own:
-        copy.wait()
+        target = peer_chip(off)
+        copy_k, copy_v = first_hop(off)
+
+        @pl.when(target > chip)
+        def _():
+            copy_k.start()
+
+        @pl.when((target > chip) & jnp.logical_not(diagonal(chip, target)))
+        def _():
+            copy_v.start()
+
+    start_all(kv_copies(k_ref, v_ref, me, sibling, 1, 0))
+
+    far_rows = wbuf.shape[1] // n_ctx
+    at_end = (rank == 0) | (rank == n_tp - 1)
+    helper = (rank == 1) | (rank == n_tp - 2)
+    inward = jnp.where(rank == 0, right, left)
+
+    def far_slice(device):
+        return w_far.at[:, pl.ds(pl.multiple_of(device * far_rows, far_rows), far_rows)]
+
+    def slice_copy():
+        first = jnp.where(rank == 0, 2, 0)
+        return pltpu.make_async_remote_copy(
+            src_ref=wbuf.at[
+                pl.ds(first, n_tp - 2),
+                pl.ds(pl.multiple_of(me * far_rows, far_rows), far_rows),
+            ],
+            dst_ref=far_slice(me),
+            send_sem=slice_send,
+            recv_sem=slice_recv,
+            device_id={"tp": inward},
+            device_id_type=MESH,
+        )
+
+    def far_copy(source, target, level, off):
+        return pltpu.make_async_remote_copy(
+            src_ref=far_slice(source),
+            dst_ref=far_slice(source),
+            send_sem=far_send.at[level, off],
+            recv_sem=far_recv.at[source],
+            device_id={"ctx": target},
+            device_id_type=MESH,
+        )
+
     for d in range(n_tp):
         pltpu.make_async_copy(
             w_hbm.at[:, pl.ds(d * width, width)], wbuf.at[d], w_sem.at[d]
         ).wait()
 
+    @pl.when(at_end)
+    def _():
+        slice_copy().start()
+
+    def relay_copy(source_chip, column):
+        source = source_chip * 2 + core
+        return pltpu.make_async_remote_copy(
+            src_ref=slot(vbuf, source),
+            dst_ref=slot(vbuf, source),
+            send_sem=relay_send.at[source_chip, column],
+            recv_sem=kv_recv.at[1, source],
+            device_id={"ctx": ((chip // side) * side + column) * 2 + core},
+            device_id_type=MESH,
+        )
+
+    def relays(off, act):
+        source_chip = lax.rem(chip + chips - off, chips)
+        for column in range(side):
+            target = (chip // side) * side + column
+
+            @pl.when(
+                (source_chip < chip) & (source_chip % side == x) & (column != x)
+                & (source_chip < target)
+            )
+            def _():
+                act(relay_copy(source_chip, column))
+
+    def forward_copies(off):
+        source = lax.rem(chip + chips - off, chips) * 2 + core
+        return kv_copies(slot(kbuf, source), slot(vbuf, source), source, sibling, 1, off)
+
+    for off in sorted(range(1, chips), key=lambda o: (-(o % side == 0), o)):
+        source_chip = lax.rem(chip + chips - off, chips)
+
+        @pl.when(source_chip < chip)
+        def _():
+            copy_k, copy_v = forward_copies(off)
+            copy_v.wait_recv()
+            copy_v.start()
+            relays(off, lambda copy: copy.start())
+            copy_k.wait_recv()
+            copy_k.start()
+
+    for off in range(chips):
+        source_chip = lax.rem(chip + chips - off, chips)
+        source = source_chip * 2 + (1 - core)
+
+        @pl.when(source_chip <= chip)
+        def _():
+            for copy in kv_copies(slot(kbuf, source), slot(vbuf, source), source, sibling, 1, off):
+                copy.wait_recv()
+
+    for copy in own:
+        copy.wait()
+
+    @pl.when(helper)
+    def _():
+        slice_copy().wait_recv()
+        for off in range(1, chips):
+            far_copy(me, peer_chip(off) * 2 + core, 0, off).start()
+        far_copy(me, sibling, 1, 0).start()
+
+    def far_forward():
+        for off in range(1, chips):
+            source = lax.rem(chip + chips - off, chips) * 2 + core
+            copy = far_copy(source, sibling, 1, off)
+            copy.wait_recv()
+            copy.start()
+
+    def far_ready():
+        for off in range(chips):
+            source = lax.rem(chip + chips - off, chips) * 2 + (1 - core)
+            far_copy(source, sibling, 1, off).wait_recv()
+
+    def att_copy(t):
+        return pltpu.make_async_remote_copy(
+            src_ref=att.at[t],
+            dst_ref=att_far.at[t],
+            send_sem=att_send.at[t],
+            recv_sem=att_recv.at[t],
+            device_id={"tp": inward},
+            device_id_type=MESH,
+        )
+
     def rs_copy(d, t, rightward):
         return pltpu.make_async_remote_copy(
             src_ref=part.at[d, t],
-            dst_ref=(from_left if rightward else from_right).at[d, t],
+            dst_ref=from_left.at[d - 1, t] if rightward else from_right.at[d, t],
             send_sem=rs_send.at[d, t],
             recv_sem=(left_recv if rightward else right_recv).at[d, t],
             device_id={"tp": right if rightward else left},
@@ -168,58 +295,106 @@
                 )
             result = (summed / total).astype(jnp.bfloat16)
             for h, lane in enumerate(lanes):
-                att[:, lane] = result[h * TILE:(h + 1) * TILE]
+                att[t, :, lane] = result[h * TILE:(h + 1) * TILE]
             return carry
 
         lax.fori_loop(0, kv_heads * pairs, unit, 0)
 
+    def raw(d, t):
+        near = jnp.where(rank == 0, d < 2, jnp.where(rank == n_tp - 1, d > n_tp - 3, True))
+        return near | (t < FIRST_FAR)
+
     def project(t):
+        @pl.when(at_end & (t >= FIRST_FAR))
+        def _():
+            att_copy(t).start()
+
         def chunk(i, carry):
             d = jnp.where(rank < n_tp // 2, n_tp - 1 - i, i)
-            part[d, t] = jnp.dot(
-                att[...], wbuf[d], preferred_element_type=jnp.float32
-            ).astype(jnp.bfloat16)
-
-            @pl.when((rank == 0) & (d > 0))
+
+            @pl.when(raw(d, t))
             def _():
-                rs_copy(d, t, True).start()
-
-            @pl.when((rank == n_tp - 1) & (d < n_tp - 1))
-            def _():
-                rs_copy(d, t, False).start()
+                part[d, t] = jnp.dot(
+                    att[t], wbuf[d], preferred_element_type=jnp.float32
+                ).astype(jnp.bfloat16)
+
+                @pl.when((rank == 0) & (d > 0))
+                def _():
+                    rs_copy(d, t, True).start()
+
+                @pl.when((rank == n_tp - 1) & (d < n_tp - 1))
+                def _():
+                    rs_copy(d, t, False).start()
 
             return carry
 
         lax.fori_loop(0, n_tp, chunk, 0)
 
-    def pass_on(t):
+    def add(d, t, other):
+        part[d, t] = (part[d, t].astype(jnp.float32) + other).astype(jnp.bfloat16)
+
+    def far_dot(j, t):
+        return jnp.dot(att_far[t], w_far[j], preferred_element_type=jnp.float32)
+
+    def await_far(t):
+        @pl.when(helper & (t >= FIRST_FAR))
+        def _():
+            att_copy(t).wait_recv()
+
+    def pass_right(t):
+        far = t >= FIRST_FAR
+
+        @pl.when(rank == 1)
+        def _():
+            await_far(t)
+
         def go_right(i, carry):
             d = n_tp - 1 - i
 
             @pl.when((d > rank) & (rank > 0))
             def _():
                 copy = rs_copy(d, t, True)
-                copy.wait_recv()
-                part[d, t] = (
-                    part[d, t].astype(jnp.float32) + from_left[d, t].astype(jnp.float32)
-                ).astype(jnp.bfloat16)
+
+                @pl.when((rank == 1) & far)
+                def _():
+                    add(d, t, far_dot(d - 2, t))
+
+                @pl.when((rank > 1) | jnp.logical_not(far))
+                def _():
+                    copy.wait_recv()
+                    add(d, t, from_left[d - 1, t].astype(jnp.float32))
+
                 copy.start()
 
             return carry
+
+        lax.fori_loop(0, n_tp, go_right, 0)
+
+    def pass_left(t):
+        far = t >= FIRST_FAR
+
+        @pl.when(rank == n_tp - 2)
+        def _():
+            await_far(t)
 
         def go_left(d, carry):
             @pl.when((d < rank) & (rank < n_tp - 1))
             def _():
                 copy = rs_copy(d, t, False)
-                copy.wait_recv()
-                part[d, t] = (
-                    part[d, t].astype(jnp.float32) + from_right[d, t].astype(jnp.float32)
-                ).astype(jnp.bfloat16)
+
+                @pl.when((rank == n_tp - 2) & far)
+                def _():
+                    add(d, t, far_dot(d, t))
+
+                @pl.when((rank < n_tp - 2) | jnp.logical_not(far))
+                def _():
+                    copy.wait_recv()
+                    add(d, t, from_right[d, t].astype(jnp.float32))
+
                 copy.start()
 
             return carry
 
-        lax.fori_loop(0, n_tp, go_right, 0)
         lax.fori_loop(0, n_tp, go_left, 0)
 
     def finish(t):
@@ -228,7 +403,7 @@
         @pl.when(rank > 0)
         def _():
             rs_copy(rank, t, True).wait_recv()
-            acc[...] += from_left[rank, t].astype(jnp.float32)
+            acc[...] += from_left[rank - 1, t].astype(jnp.float32)
 
         @pl.when(rank < n_tp - 1)
         def _():
@@ -243,30 +418,87 @@
             attend(s)
             project(s)
 
-        @pl.when((s >= 1) & (s <= tiles))
-        def _():
-            pass_on(s - 1)
-
-        @pl.when(s >= FINAL_LAG)
-        def _():
-            finish(s - FINAL_LAG)
+        @pl.when(helper & (s == FIRST_FAR))
+        def _():
+            far_forward()
+
+        @pl.when(helper & (s == FIRST_FAR + 1))
+        def _():
+            far_ready()
+
+        behind_left = s - rank
+        behind_right = s - (n_tp - 1 - rank)
+
+        @pl.when((rank > 0) & (behind_left >= 0) & (behind_left < tiles))
+        def _():
+            pass_right(behind_left)
+
+        @pl.when((rank < n_tp - 1) & (behind_right >= 0) & (behind_right < tiles))
+        def _():
+            pass_left(behind_right)
+
+        @pl.when(s >= n_tp)
+        def _():
+            finish(s - n_tp)
 
         return carry
 
-    lax.fori_loop(0, tiles + FINAL_LAG, step, 0)
+    lax.fori_loop(0, tiles + n_tp, step, 0)
 
     def drain(i, carry):
         d, t = i // tiles, i % tiles
 
-        @pl.when(d != rank)
+        @pl.when((d > rank) & raw(d, t))
         def _():
             rs_copy(d, t, True).wait_send()
 
+        @pl.when((d < rank) & raw(d, t))
+        def _():
+            rs_copy(d, t, False).wait_send()
+
         return carry
 
     lax.fori_loop(0, n_tp * tiles, drain, 0)
-    for copy in sent:
+
+    @pl.when(at_end)
+    def _():
+        slice_copy().wait_send()
+
+        def drain_att(t, carry):
+            att_copy(t).wait_send()
+            return carry
+
+        lax.fori_loop(FIRST_FAR, tiles, drain_att, 0)
+
+    @pl.when(helper)
+    def _():
+        for off in range(1, chips):
+            far_copy(me, peer_chip(off) * 2 + core, 0, off).wait_send()
+        for off in range(chips):
+            source = lax.rem(chip + chips - off, chips) * 2 + core
+            far_copy(source, sibling, 1, off).wait_send()
+
+    for off in range(1, chips):
+        target = peer_chip(off)
+        copy_k, copy_v = first_hop(off)
+
+        @pl.when(target > chip)
+        def _():
+            copy_k.wait_send()
+
+        @pl.when((target > chip) & jnp.logical_not(diagonal(chip, target)))
+        def _():
+            copy_v.wait_send()
+
+    for copy in kv_copies(k_ref, v_ref, me, sibling, 1, 0):
         copy.wait_send()
+    for off in range(1, chips):
+        @pl.when(lax.rem(chip + chips - off, chips) < chip)
+        def _():
+            for copy in forward_copies(off):
+                copy.wait_send()
+
+        relays(off, lambda copy: copy.wait_send())
 
 
 def per_device(n_ctx, n_tp, queries, keys, values, gates, out_weight):
@@ -292,10 +524,12 @@
             pltpu.VMEM((n_ctx * blocks, TOKB, kv_width), bf16),
             pltpu.VMEM((n_ctx * blocks, TOKB, kv_width), bf16),
             pltpu.VMEM((n_tp, depth, width), bf16),
-            pltpu.VMEM((TILE, q_width), bf16),
+            pltpu.VMEM((n_tp - 2, depth, width), bf16),
+            pltpu.VMEM((tiles, TILE, q_width), bf16),
+            pltpu.VMEM((tiles, TILE, q_width), bf16),
             pltpu.VMEM((n_tp, tiles, TILE, width), bf16),
-            pltpu.VMEM((n_tp, tiles, TILE, width), bf16),
-            pltpu.VMEM((n_tp, tiles, TILE, width), bf16),
+            pltpu.VMEM((n_tp - 1, tiles, TILE, width), bf16),
+            pltpu.VMEM((n_tp - 1, tiles, TILE, width), bf16),
             pltpu.VMEM((TILE, width), jnp.float32),
             pltpu.SemaphoreType.DMA((2,)),
             pltpu.SemaphoreType.DMA((n_tp,)),
@@ -304,6 +538,13 @@
             pltpu.SemaphoreType.DMA((n_tp, tiles)),
             pltpu.SemaphoreType.DMA((n_tp, tiles)),
             pltpu.SemaphoreType.DMA((n_tp, tiles)),
+            pltpu.SemaphoreType.DMA((tiles,)),
+            pltpu.SemaphoreType.DMA((tiles,)),
+            pltpu.SemaphoreType.DMA(()),
+            pltpu.SemaphoreType.DMA(()),
+            pltpu.SemaphoreType.DMA((2, chips)),
+            pltpu.SemaphoreType.DMA((n_ctx,)),
+            pltpu.SemaphoreType.DMA((chips, math.isqrt(chips))),
         ],
         compiler_params=pltpu.CompilerParams(
             collective_id=0, has_side_effects=True, vmem_limit_bytes=VMEM_LIMIT

time: 226 us -> 182 us (0.81)
  the two profiles are of different devices: /device:TPU:0 before, /device:TPU:7 now
where the time goes in v1:
time: 182 us
  Pallas kernels  177 us (97%)
  local copies, waits for them, and re-layouts  4.35 us (2%)
    pallas_call x1, Pallas kernels, per_device(): pl.pallas_call(functools.partial(kernel, n_ctx, n_tp), out_shape=jax.Shap...  177 us

profile of v1, /device:TPU:7, one launch (start us, length us, event | category | flops | bytes accessed | tf_op | source)
XLA Modules:
  0.0 181.9 jit_solution(15077287125428595465)
XLA Ops:
  0.0 1.3 reshape.18.gates_ref
  1.3 177.5 %shard_map.55 = bf16[1024,1024]{1,0:T(8,128)(2,1)} custom-call(bf16[1024,1024]{1,0:T(8,128)(2,1)} %bitcast.5, bf16[2,512,256]{2,1,0:T(8,128)(2,1)} %bitcast.6, bf16[2,512,256]{2,1,0:T(8,128)(2,1)} %bitcast.7, s32[12]{0:T(128)} %reshape.18.gates_ref, bf16[1024,4096]{1,0:T(8,128)(2,1)} %w_hbm.1), custom_call_target="tpu_custom_call" | custom-call | flops 17179869184 | bytes 11534336 | tf_op jit(solution)/shard_map/pallas_call | solution.py:514
  178.8 3.1 %copy.7 = bf16[1,1024,1024]{2,1,0:T(8,128)(2,1)} copy(bf16[1,1024,1024]{2,1,0:T(8,128)(2,1)} %bitcast.4) | data formatting | bytes 4194304
